TPU v7x, 256 devices: a whole 4x4x8 slice. The times are simulated.
256 devices in a mesh: seq: 16 (over z, x_lo), wt: 16 (over x_hi, y, core).
Axes of the slice: x: 4 (x_hi: 2, x_lo: 2; x = x_hi * 2 + x_lo), y: 4, z: 8, core: 2. Of those that a mesh axis runs over, the one named last changes fastest.
Arguments:
- frames: bfloat16 [4096, 4096], P('seq'), may hold values from -40 to 40
- attn_norm_gain: float32 [4096], replicated, may hold values from 0.1 to 1.9
- qkv_weight: bfloat16 [3, 4096, 4096], P(None, 'seq', 'wt'), may hold values from -4 to 4
- attn_out_weight: bfloat16 [4096, 4096], P('seq', 'wt'), may hold values from -0.125 to 0.125
- conv_norm_gain: float32 [4096], replicated, may hold values from 0.1 to 1.9
- glu_weight: bfloat16 [2, 4096, 4096], P(None, 'seq', 'wt'), may hold values from -0.09375 to 0.09375
- depth_kernel: float32 [31, 4096], P(None, 'wt'), may hold values from -1 to 1
- norm_scale: float32 [4096], P('wt'), may hold values from 0.5 to 2
- norm_shift: float32 [4096], P('wt'), may hold values from -3 to 3
- conv_out_weight: bfloat16 [4096, 4096], P('seq', 'wt'), may hold values from -0.125 to 0.125
Outputs:
- encoded: bfloat16 [4096, 4096], P('seq', 'wt')
All inputs are finite; a program needn't handle non-finite values.
Results may differ from a plain program's by a relative error of at most 0.014.
Values may be sent and summed in bfloat16 or wider, within the bound.
No kernel may reach another device: no remote copies, remote signals or barrier semaphores. Data moves between devices by JAX's collectives and lax.ppermute only.
A program may use at most 64 MiB of HBM per device.

v0:
```python
import jax
import jax.numpy as jnp
from jax import lax
from jax.sharding import PartitionSpec as P

HEAD_DIM = 128


def padded_2(value, sides, width):
    for axis, dim in sides:
        devices, length = (lax.axis_size(axis), value.shape[dim])
        up = [(i, (i + 1) % devices) for i in range(devices - 1)]
        down = [(j, i) for i, j in up]
        last = lax.slice_in_dim(value, length - width, length, axis=dim)
        first = lax.slice_in_dim(value, 0, width, axis=dim)
        before = lax.ppermute(last, axis, up)
        after = lax.ppermute(first, axis, down)
        value = jnp.concatenate([before, value, after], axis=dim)
    return value


def norm_rows(values, gain_vec):
    wide = values.astype(jnp.float32)
    row_mean = jnp.mean(wide, axis=-1, keepdims=True)
    centered = wide - row_mean
    row_var = jnp.mean(centered * centered, axis=-1, keepdims=True)
    return (centered * lax.rsqrt(row_var + 1e-05) * gain_vec).astype(jnp.bfloat16)


def project_in(normed, stacked):
    return jnp.einsum(
        "rd,mdc->rmc",
        normed,
        lax.all_gather(stacked, "seq", axis=1, tiled=True),
        preferred_element_type=jnp.float32,
    )


def project_out(inputs, weight):
    return lax.dot_general(
        inputs,
        lax.all_gather(weight, "seq", axis=0, tiled=True),
        (((1,), (1,)), ((), ())),
        preferred_element_type=jnp.float32,
    )


def feature_share(partial_sums):
    return lax.psum_scatter(
        partial_sums.astype(jnp.bfloat16), "wt", scatter_dimension=1, tiled=True
    ).astype(jnp.float32)


def local(
    frames,
    attn_norm_gain,
    qkv_weight,
    attn_out_weight,
    conv_norm_gain,
    glu_weight,
    depth_kernel,
    norm_scale,
    norm_shift,
    conv_out_weight,
):
    row_count = frames.shape[0]
    col_count = qkv_weight.shape[2]
    heads_here = col_count // HEAD_DIM
    column_start = lax.axis_index("wt") * col_count
    normed = norm_rows(frames, attn_norm_gain)
    projected = project_in(normed, qkv_weight).astype(jnp.bfloat16)
    query_heads = projected[:, 0].reshape(row_count, heads_here, HEAD_DIM)
    keys = projected[:, 1]
    values = projected[:, 2]
    score_scale = HEAD_DIM ** (-0.5)
    key_segment = lax.all_gather(keys, "seq", axis=0, tiled=True)
    value_segment = lax.all_gather(values, "seq", axis=0, tiled=True)
    row_best = jnp.full((heads_here, row_count), -1e30, jnp.float32)
    key_heads = key_segment.reshape(key_segment.shape[0], heads_here, HEAD_DIM)
    value_heads = value_segment.reshape(value_segment.shape[0], heads_here, HEAD_DIM)
    scores = (
        jnp.einsum("qhd,khd->hqk", query_heads, key_heads, preferred_element_type=jnp.float32)
        * score_scale
    )
    new_best = jnp.maximum(row_best, jnp.max(scores, axis=-1))
    exp_weights = jnp.exp(scores - new_best[..., None])
    running_sum = jnp.sum(exp_weights, axis=-1)
    weighted = jnp.einsum(
        "hqk,khd->hqd",
        exp_weights.astype(jnp.bfloat16),
        value_heads,
        preferred_element_type=jnp.float32,
    )
    row_best, running_sum, weighted = (new_best, running_sum, weighted)
    context = (
        (weighted / running_sum[..., None])
        .transpose(1, 0, 2)
        .reshape(row_count, col_count)
        .astype(jnp.bfloat16)
    )
    attended = project_out(context, attn_out_weight)
    share_cols = feature_share(attended)
    frame_cols = lax.dynamic_slice_in_dim(frames, column_start, col_count, 1)
    residual_cols = (frame_cols.astype(jnp.float32) + share_cols).astype(jnp.bfloat16)
    residual_full = lax.all_gather(residual_cols, "wt", axis=1, tiled=True)
    normed_conv = norm_rows(residual_full, conv_norm_gain)
    glu_pair = project_in(normed_conv, glu_weight)
    gated = (glu_pair[:, 0] * jax.nn.sigmoid(glu_pair[:, 1])).astype(jnp.bfloat16)
    rim_width = (depth_kernel.shape[0] - 1) // 2
    padded = padded_2(gated, (("seq", 0),), rim_width).astype(jnp.float32)
    depth_out = jnp.zeros((row_count, col_count), jnp.float32)
    for tap_index in range(depth_kernel.shape[0]):
        depth_out = depth_out + depth_kernel[tap_index] * padded[tap_index : tap_index + row_count]
    shifted = depth_out * norm_scale + norm_shift
    activated = (shifted * jax.nn.sigmoid(shifted)).astype(jnp.bfloat16)
    conv_cols = feature_share(project_out(activated, conv_out_weight))
    residual_cols = lax.dynamic_slice_in_dim(residual_full, column_start, col_count, 1)
    return (residual_cols.astype(jnp.float32) + conv_cols).astype(jnp.bfloat16)


def solution(mesh):
    in_specs = (
        P("seq", None),
        P(),
        P(None, "seq", "wt"),
        P("seq", "wt"),
        P(),
        P(None, "seq", "wt"),
        P(None, "wt"),
        P("wt"),
        P("wt"),
        P("seq", "wt"),
    )
    out_specs = P("seq", "wt")
    return jax.shard_map(local, mesh=mesh, in_specs=in_specs, out_specs=out_specs, check_vma=False)
```

profile of v0, /device:TPU:32, one launch (start us, length us, event | category | flops | bytes accessed | tf_op | source)
XLA Modules:
  0.0 819.5 jit_solution(16398674720940230616)
XLA Ops:
  6.5 2.1 copy.11
  8.7 2.0 convert_reduce_fusion.1
  11.4 156.5 %all-gather.10.cloned.1.call-done = bf16[3,4096,256]{1,2,0:T(8,128)(2,1)} async-done(((bf16[3,256,256]{1,2,0:T(8,128)(2,1)}), bf16[3,4096,256]{1,2,0:T(8,128)(2,1)}) %all-gather.10.cloned.1.call-update) | async-done | bytes 6291472 | tf_op jit(solution)/shard_map/all_gather | solution.py:34
  167.9 4.7 fusion.28
  174.7 85.2 %all-gather.20.cloned.1.call-done = bf16[4096,1,256]{0,2,1:T(8,128)(2,1)} async-done(((bf16[256,1,256]{0,2,1:T(8,128)(2,1)}), bf16[4096,1,256]{0,2,1:T(8,128)(2,1)}) %all-gather.20.cloned.1.call-update) | async-done | bytes 2097168 | tf_op jit(solution)/shard_map/all_gather | solution.py:76
  260.0 3.0 multiply_reduce_fusion
  263.0 3.2 copy-done
  267.7 77.6 %all-gather.22.cloned.1.call-done = bf16[4096,1,256]{0,2,1:T(8,128)(2,1)} async-done(((bf16[256,1,256]{0,2,1:T(8,128)(2,1)}), bf16[4096,1,256]{0,2,1:T(8,128)(2,1)}) %all-gather.22.cloned.1.call-update) | async-done | bytes 2097168 | tf_op jit(solution)/shard_map/all_gather | solution.py:77
  345.3 5.8 fusion.37
  351.1 69.0 %all-gather.12.cloned.1.call-done = bf16[4096,256]{1,0:T(8,128)(2,1)} async-done(((bf16[256,256]{1,0:T(8,128)(2,1)}), bf16[4096,256]{1,0:T(8,128)(2,1)}) %all-gather.12.cloned.1.call-update) | async-done | bytes 2097168 | tf_op jit(solution)/shard_map/all_gather | solution.py:42
  420.2 3.7 convolution_convert_fusion.1
  423.9 77.6 %reduce-scatter.3.cloned.1.call-done = bf16[256,256]{1,0:T(8,128)(2,1)} async-done(((bf16[256,4096]{1,0:T(8,128)(2,1)}), bf16[256,256]{1,0:T(8,128)(2,1)}) %reduce-scatter.3.cloned.1.call-update) | async-done | bytes 131088 | tf_op jit(solution)/shard_map/reduce_scatter | solution.py:49
  501.5 1.6 add_convert_fusion.1
  504.7 50.7 %all-gather.14.cloned.1.call-done = bf16[256,4096]{1,0:T(8,128)(2,1)} async-done(((bf16[256,256]{1,0:T(8,128)(2,1)}), bf16[256,4096]{1,0:T(8,128)(2,1)}) %all-gather.14.cloned.1.call-update) | async-done | bytes 2097168 | tf_op jit(solution)/shard_map/all_gather | solution.py:105
  555.5 2.1 convert_reduce_fusion
  557.6 2.3 fusion.6
  559.9 94.7 %all-gather.16.cloned.1.call-done = bf16[2,4096,256]{2,1,0:T(8,128)(2,1)} async-done(((bf16[2,256,256]{2,1,0:T(8,128)(2,1)}), bf16[2,4096,256]{2,1,0:T(8,128)(2,1)}) %all-gather.16.cloned.1.call-update) | async-done | bytes 4194320 | tf_op jit(solution)/shard_map/all_gather | solution.py:34
  654.6 3.5 fusion.20
  658.2 3.9 collective-permute-start
  662.0 2.9 collective-permute-start.1
  665.0 2.6 collective-permute-done.1
  667.6 61.0 %all-gather.18.cloned.1.call-done = bf16[4096,256]{1,0:T(8,128)(2,1)} async-done(((bf16[256,256]{1,0:T(8,128)(2,1)}), bf16[4096,256]{1,0:T(8,128)(2,1)}) %all-gather.18.cloned.1.call-update) | async-done | bytes 2097168 | tf_op jit(solution)/shard_map/all_gather | solution.py:42
  728.6 4.6 convolution_convert_fusion
  733.2 78.1 %reduce-scatter.5.cloned.1.call-done = bf16[256,256]{1,0:T(8,128)(2,1)} async-done(((bf16[256,4096]{1,0:T(8,128)(2,1)}), bf16[256,256]{1,0:T(8,128)(2,1)}) %reduce-scatter.5.cloned.1.call-update) | async-done | bytes 131088 | tf_op jit(solution)/shard_map/reduce_scatter | solution.py:49
  (49 shorter events, 7.8 us)
Async XLA Ops:
  6.5 4.1 copy-start.1
  6.5 161.3 %copy-start.4 = (f32[4096]{0:T(1024)S(1)}, f32[4096]{0:T(1024)}, u32[]{:S(2)}) copy-start(f32[4096]{0:T(1024)} %param.11) | copy-start | bytes 49156
  6.5 161.3 %all-gather.10.cloned.1.call-start = ((), (), s32[]{:S(2)}) async-start(), calls=%async_computation.2 | async-start | bytes 6684672 | tf_op jit(solution)/shard_map/all_gather | solution.py:34
  8.6 251.3 %all-gather.20.cloned.1.call-start = ((), (), s32[]{:S(2)}) async-start(), calls=%async_computation.9 | async-start | bytes 2228224 | tf_op jit(solution)/shard_map/all_gather | solution.py:76
  173.4 172.0 %all-gather.22.cloned.1.call-start = ((), (), s32[]{:S(2)}) async-start(), calls=%async_computation.10 | async-start | bytes 2228224 | tf_op jit(solution)/shard_map/all_gather | solution.py:77
  174.1 246.1 %all-gather.12.cloned.1.call-start = ((), (), s32[]{:S(2)}) async-start(), calls=%async_computation.3 | async-start | bytes 2228224 | tf_op jit(solution)/shard_map/all_gather | solution.py:42
  174.7 326.9 %reduce-scatter.3.cloned.1.call-start = ((), (), s32[]{:S(2)}) async-start(), calls=%async_computation.4 | async-start | bytes 2228224 | tf_op jit(solution)/shard_map/reduce_scatter | solution.py:49
  262.9 3.2 copy-start
  351.1 153.6 %copy-start.3 = (f32[31,256]{1,0:T(8,128)S(1)}, f32[31,256]{1,0:T(8,128)}, u32[]{:S(2)}) copy-start(f32[31,256]{1,0:T(8,128)} %param.16) | copy-start | bytes 95236
  423.9 230.7 %copy-start.5 = (f32[4096]{0:T(1024)S(1)}, f32[4096]{0:T(1024)}, u32[]{:S(2)}) copy-start(f32[4096]{0:T(1024)} %param.14) | copy-start | bytes 49156
  423.9 131.6 %all-gather.14.cloned.1.call-start = ((), (), s32[]{:S(2)}) async-start(), calls=%async_computation.5 | async-start | bytes 2228224 | tf_op jit(solution)/shard_map/all_gather | solution.py:105
  503.1 151.4 %all-gather.16.cloned.1.call-start = ((), (), s32[]{:S(2)}) async-start(), calls=%async_computation.6 | async-start | bytes 4456448 | tf_op jit(solution)/shard_map/all_gather | solution.py:34
  503.9 224.7 %all-gather.18.cloned.1.call-start = ((), (), s32[]{:S(2)}) async-start(), calls=%async_computation.7 | async-start | bytes 2228224 | tf_op jit(solution)/shard_map/all_gather | solution.py:42
  504.6 306.7 %reduce-scatter.5.cloned.1.call-start = ((), (), s32[]{:S(2)}) async-start(), calls=%async_computation.8 | async-start | bytes 2228224 | tf_op jit(solution)/shard_map/reduce_scatter | solution.py:49
  555.5 99.1 %copy-start.2 = (bf16[256,4096]{1,0:T(8,128)(2,1)S(1)}, bf16[256,4096]{1,0:T(8,128)(2,1)}, u32[]{:S(2)}) copy-start(bf16[256,4096]{1,0:T(8,128)(2,1)} %all-gather.14.cloned.1.call-done) | copy-start | bytes 6291460
  559.9 168.8 %copy-start.6 = (f32[256]{0:T(256)S(1)}, f32[256]{0:T(256)}, u32[]{:S(2)}) copy-start(f32[256]{0:T(256)} %param.18) | copy-start | bytes 3076
  559.9 168.7 %copy-start.7 = (f32[256]{0:T(256)S(1)}, f32[256]{0:T(256)}, u32[]{:S(2)}) copy-start(f32[256]{0:T(256)} %param.17) | copy-start | bytes 3076
  658.2 6.8 collective-permute-start
  662.0 5.5 collective-permute-start.1
Sparse Core Ops, SparseCore 0:
  9.1 158.7 all-gather.9
  173.5 86.4 all-gather.19
  261.7 83.6 all-gather.21
  347.0 73.1 all-gather.11
  424.2 77.2 reduce-scatter.2
  504.3 51.1 all-gather.13
  557.4 97.1 all-gather.15
  656.5 72.0 all-gather.17
  733.4 77.9 reduce-scatter.4
where the time goes:
time: 820 us; the launch traced here: 819 us
  waiting for transfers between devices  756 us (92%)
  matrix products  25.2 us (3%)
  between operations  13.4 us (2%)
  other arithmetic  11.9 us (1%)
    all_gather x2, waiting for transfers between devices, project_in(): lax.all_gather(stacked, 'seq', axis=1, tiled=True)  251 us
    reduce_scatter x2, waiting for transfers between devices, feature_share(): lax.psum_scatter(partial_sums.astype(jnp.bfloat16), 'wt', scatter_dimensi...  156 us
    all_gather x2, waiting for transfers between devices, project_out(): lax.all_gather(weight, 'seq', axis=0, tiled=True)  130 us
    all_gather x1, waiting for transfers between devices, local(): key_segment = lax.all_gather(keys, 'seq', axis=0, tiled=True)  85.2 us
    all_gather x1, waiting for transfers between devices, local(): value_segment = lax.all_gather(values, 'seq', axis=0, tiled=True)  77.6 us
    all_gather x1, waiting for transfers between devices, local(): residual_full = lax.all_gather(residual_cols, 'wt', axis=1, tiled=True)  50.7 us
  transfers between devices with their start and end apart: 11, of which 10 were waited for; matrix products, arithmetic and copies ran while one was open for 3% of the time, Pallas kernels for 0%

commit v1 on v0

--- a/solution.py
+++ b/solution.py
@@ -73,7 +73,15 @@
     keys = projected[:, 1]
     values = projected[:, 2]
     score_scale = HEAD_DIM ** (-0.5)
-    key_segment = lax.all_gather(keys, "seq", axis=0, tiled=True)
+    key_segment = jnp.concatenate(
+        lax.all_to_all(
+            jnp.stack(lax.axis_size("seq") * [keys], axis=0),
+            axis_name="seq",
+            split_axis=0,
+            concat_axis=0,
+        ),
+        0,
+    )
     value_segment = lax.all_gather(values, "seq", axis=0, tiled=True)
     row_best = jnp.full((heads_here, row_count), -1e30, jnp.float32)
     key_heads = key_segment.reshape(key_segment.shape[0], heads_here, HEAD_DIM)

time: 820 us -> 760 us (0.927)
  waiting for transfers between devices: 756 us -> 679 us
  local copies, waits for them, and re-layouts: 6.1 us -> 15.9 us
    all_gather x1 -> x0, waiting for transfers between devices: 85.2 us -> none  [local(): key_segment = lax.all_gather(keys, 'seq', axis=0, tiled=True)]
    all_to_all x0 -> x1, waiting for transfers between devices: none -> 49.5 us  [local(): lax.all_to_all(jnp.stack(lax.axis_size('seq') * [keys], axis=0), axis_nam...]
    all_gather x1, waiting for transfers between devices: 77.6 us -> 35.2 us  [local(): value_segment = lax.all_gather(values, 'seq', axis=0, tiled=True)]
  transfers between devices with their start and end apart: 11 -> 11, of which waited for: 10 -> 10; matrix products, arithmetic and copies ran while one was open for 3% -> 4% of each run, Pallas kernels for 0% -> 0%
where the time goes in v1:
time: 760 us; the launch traced here: 759 us
  waiting for transfers between devices  679 us (89%)
  matrix products  25.2 us (3%)
  local copies, waits for them, and re-layouts  15.9 us (2%)
  between operations  13.7 us (2%)
  starting transfers between devices  13.4 us (2%)
  other arithmetic  11.9 us (2%)
    all_gather x2, waiting for transfers between devices, project_in(): lax.all_gather(stacked, 'seq', axis=1, tiled=True)  251 us
    reduce_scatter x2, waiting for transfers between devices, feature_share(): lax.psum_scatter(partial_sums.astype(jnp.bfloat16), 'wt', scatter_dimensi...  156 us
    all_gather x2, waiting for transfers between devices, project_out(): lax.all_gather(weight, 'seq', axis=0, tiled=True)  133 us
    all_gather x1, waiting for transfers between devices, local(): residual_full = lax.all_gather(residual_cols, 'wt', axis=1, tiled=True)  50.7 us
    all_to_all x1, waiting for transfers between devices, local(): lax.all_to_all(jnp.stack(lax.axis_size('seq') * [keys], axis=0), axis_nam...  49.5 us
    all_gather x1, waiting for transfers between devices, local(): value_segment = lax.all_gather(values, 'seq', axis=0, tiled=True)  35.2 us
  transfers between devices with their start and end apart: 11, of which 10 were waited for; matrix products, arithmetic and copies ran while one was open for 4% of the time, Pallas kernels for 0%

profile of v1, /device:TPU:32, one launch (start us, length us, event | category | flops | bytes accessed | tf_op | source)
XLA Modules:
  0.0 759.3 jit_solution(1842699147005935059)
XLA Ops:
  11.4 156.5 %all-gather.8.cloned.1.call-done = bf16[3,4096,256]{1,2,0:T(8,128)(2,1)} async-done(((bf16[3,256,256]{1,2,0:T(8,128)(2,1)}), bf16[3,4096,256]{1,2,0:T(8,128)(2,1)}) %all-gather.8.cloned.1.call-update) | async-done | bytes 6291472 | tf_op jit(solution)/shard_map/all_gather | solution.py:34
  167.9 4.7 fusion.28
  174.8 6.2 all-to-all-start
  181.8 49.5 %all-to-all-done = bf16[16,256,256]{1,2,0:T(8,128)(2,1)} async-done(((bf16[16,256,256]{1,2,0:T(8,128)(2,1)}), bf16[16,256,256]{1,2,0:T(8,128)(2,1)}, u32[]{:S(2)}, u32[]{:S(2)}) %all-to-all-start) | async-done | bytes 2097184 | tf_op jit(solution)/shard_map/all_to_all | solution.py:77
  231.3 4.1 copy.18
  235.4 4.2 reshape_reshape.3
  239.6 3.0 multiply_reduce_fusion
  242.7 3.2 copy-done
  247.4 35.2 %all-gather.18.cloned.1.call-done = bf16[4096,1,256]{0,2,1:T(8,128)(2,1)} async-done(((bf16[256,1,256]{0,2,1:T(8,128)(2,1)}), bf16[4096,1,256]{0,2,1:T(8,128)(2,1)}) %all-gather.18.cloned.1.call-update) | async-done | bytes 2097168 | tf_op jit(solution)/shard_map/all_gather | solution.py:85
  282.6 5.8 fusion.37
  288.4 71.5 %all-gather.10.cloned.1.call-done = bf16[4096,256]{1,0:T(8,128)(2,1)} async-done(((bf16[256,256]{1,0:T(8,128)(2,1)}), bf16[4096,256]{1,0:T(8,128)(2,1)}) %all-gather.10.cloned.1.call-update) | async-done | bytes 2097168 | tf_op jit(solution)/shard_map/all_gather | solution.py:42
  359.9 3.7 convolution_convert_fusion.1
  363.7 77.6 %reduce-scatter.3.cloned.1.call-done = bf16[256,256]{1,0:T(8,128)(2,1)} async-done(((bf16[256,4096]{1,0:T(8,128)(2,1)}), bf16[256,256]{1,0:T(8,128)(2,1)}) %reduce-scatter.3.cloned.1.call-update) | async-done | bytes 131088 | tf_op jit(solution)/shard_map/reduce_scatter | solution.py:49
  444.5 50.7 %all-gather.12.cloned.1.call-done = bf16[256,4096]{1,0:T(8,128)(2,1)} async-done(((bf16[256,256]{1,0:T(8,128)(2,1)}), bf16[256,4096]{1,0:T(8,128)(2,1)}) %all-gather.12.cloned.1.call-update) | async-done | bytes 2097168 | tf_op jit(solution)/shard_map/all_gather | solution.py:113
  495.2 2.1 convert_reduce_fusion
  497.3 2.3 fusion.6
  499.6 94.5 %all-gather.14.cloned.1.call-done = bf16[2,4096,256]{2,1,0:T(8,128)(2,1)} async-done(((bf16[2,256,256]{2,1,0:T(8,128)(2,1)}), bf16[2,4096,256]{2,1,0:T(8,128)(2,1)}) %all-gather.14.cloned.1.call-update) | async-done | bytes 4194320 | tf_op jit(solution)/shard_map/all_gather | solution.py:34
  594.2 3.5 fusion.20
  597.7 3.9 collective-permute-start
  601.6 2.9 collective-permute-start.1
  604.6 2.5 collective-permute-done.1
  607.2 61.0 %all-gather.16.cloned.1.call-done = bf16[4096,256]{1,0:T(8,128)(2,1)} async-done(((bf16[256,256]{1,0:T(8,128)(2,1)}), bf16[4096,256]{1,0:T(8,128)(2,1)}) %all-gather.16.cloned.1.call-update) | async-done | bytes 2097168 | tf_op jit(solution)/shard_map/all_gather | solution.py:42
  668.2 4.6 convolution_convert_fusion
  672.8 78.1 %reduce-scatter.5.cloned.1.call-done = bf16[256,256]{1,0:T(8,128)(2,1)} async-done(((bf16[256,4096]{1,0:T(8,128)(2,1)}), bf16[256,256]{1,0:T(8,128)(2,1)}) %reduce-scatter.5.cloned.1.call-update) | async-done | bytes 131088 | tf_op jit(solution)/shard_map/reduce_scatter | solution.py:49
  (51 shorter events, 14.4 us)
Async XLA Ops:
  6.5 4.1 copy-start.1
  6.5 161.3 %copy-start.4 = (f32[4096]{0:T(1024)S(1)}, f32[4096]{0:T(1024)}, u32[]{:S(2)}) copy-start(f32[4096]{0:T(1024)} %param.11) | copy-start | bytes 49156
  6.5 161.3 %all-gather.8.cloned.1.call-start = ((), (), s32[]{:S(2)}) async-start(), calls=%async_computation.3 | async-start | bytes 6684672 | tf_op jit(solution)/shard_map/all_gather | solution.py:34
  8.7 274.0 %all-gather.18.cloned.1.call-start = ((), (), s32[]{:S(2)}) async-start(), calls=%async_computation.10 | async-start | bytes 2228224 | tf_op jit(solution)/shard_map/all_gather | solution.py:85
  174.8 56.5 %all-to-all-start = ((bf16[16,256,256]{1,2,0:T(8,128)(2,1)}), bf16[16,256,256]{1,2,0:T(8,128)(2,1)}, u32[]{:S(2)}, u32[]{:S(2)}) async-start(bf16[16,256,256]{1,2,0:T(8,128)(2,1)} %stack.3), calls=%async_computation | async-start | bytes 4194304 | tf_op jit(solution)/shard_map/all_to_all | solution.py:77
  181.0 178.9 %all-gather.10.cloned.1.call-start = ((), (), s32[]{:S(2)}) async-start(), calls=%async_computation.4 | async-start | bytes 2228224 | tf_op jit(solution)/shard_map/all_gather | solution.py:42
  181.8 259.5 %reduce-scatter.3.cloned.1.call-start = ((), (), s32[]{:S(2)}) async-start(), calls=%async_computation.5 | async-start | bytes 2228224 | tf_op jit(solution)/shard_map/reduce_scatter | solution.py:49
  242.6 3.2 copy-start
  288.4 156.1 %copy-start.3 = (f32[31,256]{1,0:T(8,128)S(1)}, f32[31,256]{1,0:T(8,128)}, u32[]{:S(2)}) copy-start(f32[31,256]{1,0:T(8,128)} %param.16) | copy-start | bytes 95236
  363.6 230.5 %copy-start.5 = (f32[4096]{0:T(1024)S(1)}, f32[4096]{0:T(1024)}, u32[]{:S(2)}) copy-start(f32[4096]{0:T(1024)} %param.14) | copy-start | bytes 49156
  363.6 131.6 %all-gather.12.cloned.1.call-start = ((), (), s32[]{:S(2)}) async-start(), calls=%async_computation.6 | async-start | bytes 2228224 | tf_op jit(solution)/shard_map/all_gather | solution.py:113
  442.9 151.2 %all-gather.14.cloned.1.call-start = ((), (), s32[]{:S(2)}) async-start(), calls=%async_computation.7 | async-start | bytes 4456448 | tf_op jit(solution)/shard_map/all_gather | solution.py:34
  443.5 224.7 %all-gather.16.cloned.1.call-start = ((), (), s32[]{:S(2)}) async-start(), calls=%async_computation.8 | async-start | bytes 2228224 | tf_op jit(solution)/shard_map/all_gather | solution.py:42
  444.2 306.7 %reduce-scatter.5.cloned.1.call-start = ((), (), s32[]{:S(2)}) async-start(), calls=%async_computation.9 | async-start | bytes 2228224 | tf_op jit(solution)/shard_map/reduce_scatter | solution.py:49
  495.2 99.0 %copy-start.2 = (bf16[256,4096]{1,0:T(8,128)(2,1)S(1)}, bf16[256,4096]{1,0:T(8,128)(2,1)}, u32[]{:S(2)}) copy-start(bf16[256,4096]{1,0:T(8,128)(2,1)} %all-gather.12.cloned.1.call-done) | copy-start | bytes 6291460
  499.6 168.6 %copy-start.6 = (f32[256]{0:T(256)S(1)}, f32[256]{0:T(256)}, u32[]{:S(2)}) copy-start(f32[256]{0:T(256)} %param.18) | copy-start | bytes 3076
  499.6 168.6 %copy-start.7 = (f32[256]{0:T(256)S(1)}, f32[256]{0:T(256)}, u32[]{:S(2)}) copy-start(f32[256]{0:T(256)} %param.17) | copy-start | bytes 3076
  597.7 6.8 collective-permute-start
  601.6 5.5 collective-permute-start.1
Sparse Core Ops, SparseCore 0:
  9.1 158.7 all-gather.7
  173.4 109.1 all-gather.17
  284.4 75.4 all-gather.9
  363.9 77.3 reduce-scatter.2
  444.0 51.1 all-gather.11
  497.0 97.1 all-gather.13
  596.1 72.0 all-gather.15
  673.0 77.8 reduce-scatter.4
